TPU v7x, 512 devices: a whole 4x8x8 slice. The times are simulated.
512 devices in a mesh: expert: 64 (over y_hi, z, x), fsdp: 8 (over y_lo, core).
Axes of the slice: x: 4, y: 8 (y_hi: 2, y_lo: 4; y = y_hi * 4 + y_lo), z: 8, core: 2. Of those that a mesh axis runs over, the one named last changes fastest.
Arguments:
- expert_weights: bfloat16 [64, 7168, 1024], P(None, 'expert', 'fsdp'), may hold values from -0.0625 to 0.0625
- kv_up_weight: bfloat16 [512, 32768], P('fsdp', 'expert'), may hold values from -8 to 8
- owner_table: int32 [256], replicated, may hold values from 0 to 63, as said below
- moved_experts: int32 [64], replicated, may hold values from 0 to 255, as said below
Outputs:
- expert_values: bfloat16 [64, 7168, 1024], P('expert', None, 'fsdp')
- expert_scales: float32 [64, 56, 8], P('expert', None, 'fsdp')
- mla_values: bfloat16 [512, 32768], P(None, 'expert')
- mla_scales: float32 [4, 256], P(None, 'expert')
Inputs may be any that keep to these rules, and one draw needn't show every extreme that they name: For every owner i from 0 to 63, exactly 1 of the experts named in moved_experts have owner_table value i; other entries are any owner. `moved_experts`: distinct layer expert numbers.
All inputs are finite; a program needn't handle non-finite values.
Results may differ from a plain program's by a relative error of at most 0.0045.
Values may be sent and summed in bfloat16 or wider, within the bound.
A program may use at most 64 MiB of HBM per device.

v0:
```python
import jax
import jax.numpy as jnp
from jax import lax
from jax.sharding import PartitionSpec as P

BLOCK = 128


EPSILON = 1e-06


def block_maxima(values, row_block, col_block):
    dims_in = values.shape
    folded = jnp.abs(values).reshape(
        dims_in[:-2] + (dims_in[-2] // row_block, row_block, dims_in[-1] // col_block, col_block)
    )
    return jnp.max(folded, axis=(-3, -1))


def divide_blocks(values, scales, row_block, col_block):
    dims_in = values.shape
    folded = values.reshape(
        dims_in[:-2] + (dims_in[-2] // row_block, row_block, dims_in[-1] // col_block, col_block)
    )
    return (folded / scales[..., :, None, :, None]).reshape(dims_in).astype(jnp.bfloat16)


def requantize(values, row_block, col_block):
    scales = block_maxima(values, row_block, col_block) + EPSILON
    return (divide_blocks(values, scales, row_block, col_block), scales)


def on_device(expert_weights, kv_up_weight, owner_table, moved_experts):
    moved_count = expert_weights.shape[0]
    owners = jnp.take(owner_table, moved_experts)
    sort_keys = owners * moved_count + jnp.arange(moved_count, dtype=jnp.int32)
    ranking = jnp.argsort(sort_keys)
    ordered = jnp.take(expert_weights, ranking, axis=0)
    arrived = lax.all_to_all(ordered, "expert", split_axis=0, concat_axis=1, tiled=True)
    expert_values, expert_scales = requantize(arrived.astype(jnp.float32), BLOCK, BLOCK)
    gathered = lax.all_gather(kv_up_weight, "fsdp", axis=0, tiled=True)
    mla_values, mla_scales = requantize(gathered.astype(jnp.float32), BLOCK, BLOCK)
    return (expert_values, expert_scales, mla_values, mla_scales)


def solution(mesh):
    in_specs = (P(None, "expert", "fsdp"), P("fsdp", "expert"), P(), P())
    out_specs = (
        P("expert", None, "fsdp"),
        P("expert", None, "fsdp"),
        P(None, "expert"),
        P(None, "expert"),
    )
    return jax.shard_map(
        on_device, mesh=mesh, in_specs=in_specs, out_specs=out_specs, check_vma=False
    )
```

profile of v0, /device:TPU:129, one launch (start us, length us, event | category | flops | bytes accessed | tf_op | source)
XLA Modules:
  0.0 96.3 jit_solution(15393029152468761574)
XLA Ops:
  0.6 0.0 copy-start
  0.6 0.8 compare_select_fusion.1
  1.4 1.5 %gather_fusion = s32[64]{0:T(128)S(1)} fusion(s32[256]{0:T(256)} %param.6, s32[1024]{0:T(1024)S(1)} %pad_clamp_fusion.1), kind=kCustom, calls=%fused_computation | custom fusion | bytes 768 | tf_op jit(solution)/shard_map/jit(_take)/gather | solution.py:35
  2.9 0.7 iota_add_fusion
  3.6 2.0 %sort.17 = (s32[64]{0:T(128)}, s32[64]{0:T(128)S(1)}) sort(s32[64]{0:T(128)S(1)} %iota_add_fusion, s32[64]{0:T(128)S(1)} %iota.8), dimensions={0}, to_apply=%region_0.1 | sort | flops 384 | bytes 1024 | tf_op jit(solution)/shard_map/jit(argsort)/sort | solution.py:37
  5.6 0.0 copy-done
  5.7 2.0 %gather_fusion.1 = bf16[64,112,128]{2,1,0:T(8,128)(2,1)} fusion(bf16[64,112,128]{2,1,0:T(8,128)(2,1)S(1)} %copy-done, s32[1024]{0:T(1024)S(1)} %pad_clamp_fusion), kind=kCustom, calls=%fused_computation.1 | custom fusion | bytes 3670272 | tf_op jit(solution)/shard_map/jit(_take)/gather | solution.py:38
  7.7 3.0 %broadcast_select_fusion = bf16[64,112,128]{2,1,0:T(8,128)(2,1)} fusion(bf16[64,112,128]{2,1,0:T(8,128)(2,1)} %gather_fusion.1, pred[64]{0:T(512)(128)(4,1)S(1)} %compare_and_fusion), kind=kLoop, calls=%fused_computation.5 | loop fusion | flops 917504 | bytes 3670080 | tf_op jit(solution)/shard_map/jit(_take)/select_n | solution.py:38
  10.6 17.1 %all-to-all-start = ((bf16[64,112,128]{2,1,0:T(8,128)(2,1)}), bf16[64,112,128]{2,1,0:T(8,128)(2,1)}, u32[]{:S(2)}, u32[]{:S(2)}) async-start(bf16[64,112,128]{2,1,0:T(8,128)(2,1)} %broadcast_select_fusion), calls=%async_computation | async-start | bytes 3670016 | tf_op jit(solution)/shard_map/all_to_all | solution.py:39
  27.7 0.0 copy-done.1
  27.7 55.6 %all_gather.3 = bf16[512,512]{1,0:T(8,128)(2,1)S(1)} all-gather(bf16[64,512]{1,0:T(8,128)(2,1)S(1)} %copy-done.1), channel_id=1, replica_groups=mesh['expert'=64,'fsdp'=8] {'fsdp'}, dimensions={0}, use_global_device_ids=true | all-gather | bytes 589824 | tf_op jit(solution)/shard_map/all_gather | solution.py:41
  83.4 1.1 %convert_abs_fusion = f32[512,512]{1,0:T(8,128)} fusion(bf16[512,512]{1,0:T(8,128)(2,1)S(1)} %all_gather.3), kind=kLoop, calls=%fused_computation.7 | loop fusion | flops 524288 | bytes 1572864 | tf_op jit(solution)/shard_map/abs | solution.py:14
  84.5 1.6 %reshape.116 = f32[4,128,4,128]{3,2,1,0:T(4,128)S(1)} reshape(f32[512,512]{1,0:T(8,128)} %convert_abs_fusion) | data formatting | bytes 2097152 | tf_op jit(solution)/shard_map/reshape | solution.py:14
  86.1 0.3 reduce_max.28
  86.4 0.2 div.37
  86.6 1.0 %fusion.1 = bf16[512,512]{1,0:T(8,128)(2,1)} fusion(bf16[512,512]{1,0:T(8,128)(2,1)S(1)} %all_gather.3, f32[64,8,4,128]{3,2,1,0:T(4,128)S(1)} %bitcast.14), kind=kLoop, calls=%fused_computation.8 | loop fusion | flops 786432 | bytes 2097152 | tf_op jit(solution)/shard_map/convert_element_type | solution.py:25
  87.6 0.0 all-to-all-done
  87.6 2.2 %abs_reduce_fusion = f32[64,112]{1,0:T(8,128)S(1)} fusion(bf16[64,112,128]{2,1,0:T(8,128)(2,1)} %all-to-all-done), kind=kLoop, calls=%fused_computation.4 | loop fusion | flops 2745344 | bytes 1863680 | tf_op jit(solution)/shard_map/reduce_max | solution.py:17
  89.8 0.1 reduce_max.26
  89.9 0.1 reduce_max.27
  90.0 0.5 fusion.2
  90.5 0.1 broadcast_bitcast_fusion
  90.6 1.8 %convert_element_type.47 = f32[64,112,128]{2,1,0:T(8,128)S(1)} convert(bf16[64,112,128]{2,1,0:T(8,128)(2,1)} %all-to-all-done) | non-fusion elementwise | flops 917504 | bytes 5505024 | tf_op jit(solution)/shard_map/convert_element_type | solution.py:40
  92.3 3.9 %fusion = bf16[1,7168,128]{2,1,0:T(8,128)(2,1)} fusion(f32[7168]{0:T(1024)S(1)} %broadcast_bitcast_fusion, f32[1,7168,128]{2,1,0:T(8,128)S(1)} %bitcast.13), kind=kLoop, calls=%fused_computation.3 | loop fusion | flops 1835008 | bytes 5533696 | tf_op jit(solution)/shard_map/convert_element_type | solution.py:25
  (9 shorter events, 0.0 us)
Async XLA Ops:
  0.6 5.0 %copy-start = (bf16[64,112,128]{2,1,0:T(8,128)(2,1)S(1)}, bf16[64,112,128]{2,1,0:T(8,128)(2,1)}, u32[]{:S(2)}) copy-start(bf16[64,112,128]{2,1,0:T(8,128)(2,1)} %param.4) | copy-start | bytes 5505028
  10.6 17.1 %copy-start.1 = (bf16[64,512]{1,0:T(8,128)(2,1)S(1)}, bf16[64,512]{1,0:T(8,128)(2,1)}, u32[]{:S(2)}) copy-start(bf16[64,512]{1,0:T(8,128)(2,1)} %param.5) | copy-start | bytes 196612
  10.6 77.0 %all-to-all-start = ((bf16[64,112,128]{2,1,0:T(8,128)(2,1)}), bf16[64,112,128]{2,1,0:T(8,128)(2,1)}, u32[]{:S(2)}, u32[]{:S(2)}) async-start(bf16[64,112,128]{2,1,0:T(8,128)(2,1)} %broadcast_select_fusion), calls=%async_computation | async-start | bytes 3670016 | tf_op jit(solution)/shard_map/all_to_all | solution.py:39
  86.4 3.4 %copy-start.2 = (f32[4,4]{1,0:T(4,128)}, f32[4,4]{1,0:T(4,128)S(1)}, u32[]{:S(2)}) copy-start(f32[4,4]{1,0:T(4,128)S(1)} %broadcast_add_fusion) | copy-start | bytes 196
where the time goes:
time: 96.7 us; the launch traced here: 96.3 us
  blocking collectives  55.6 us (57%)
  other arithmetic  17.4 us (18%)
  starting transfers between devices  17.1 us (18%)
  local copies, waits for them, and re-layouts  5.43 us (6%)
    all_gather x1, blocking collectives, on_device(): gathered = lax.all_gather(kv_up_weight, 'fsdp', axis=0, tiled=True)  55.6 us
    all_to_all x1, starting transfers between devices, on_device(): lax.all_to_all(ordered, 'expert', split_axis=0, concat_axis=1, tiled=True)  17.1 us
    convert_element_type x2, other arithmetic, divide_blocks(): (folded / scales[..., :, None, :, None]).reshape(dims_in)  4.94 us
    select_n x2, other arithmetic, on_device(): ordered = jnp.take(expert_weights, ranking, axis=0)  2.96 us
    reduce_max x3, other arithmetic, block_maxima(): return jnp.max(folded, axis=(-3, -1))  2.56 us
    sort x1, other arithmetic, on_device(): ranking = jnp.argsort(sort_keys)  2.04 us
    gather x1, local copies, waits for them, and re-layouts, on_device(): ordered = jnp.take(expert_weights, ranking, axis=0)  2.02 us
  transfers between devices with their start and end apart: 1, of which 0 were waited for; matrix products, arithmetic and copies ran while one was open for 4% of the time, Pallas kernels for 0%

commit v1 on v0

v1 whole, which is shorter than its diff:
```python
import functools

import jax
import jax.numpy as jnp
from jax import lax
from jax.experimental import pallas as pl
from jax.experimental.pallas import tpu as pltpu
from jax.sharding import PartitionSpec as P

MESH = pl.DeviceIdType.MESH
BLOCK = 128
EPSILON = 1e-06
Y_HI, Z, X = 2, 8, 4
Y_LO, CORE = 4, 2
RING_LINKS = ("y+", "y-", "z+", "z-", "x+", "x-")


def link_loads(offset):
    dy, dz, dx = offset
    loads = dict.fromkeys(RING_LINKS, 0)
    if dy:
        loads["y+"] = loads["y-"] = 2
    if dz == Z // 2:
        loads["z+"] = loads["z-"] = 2
    elif dz:
        loads["z+" if dz < Z // 2 else "z-"] = min(dz, Z - dz)
    if dx == X // 2:
        loads["x+"] = loads["x-"] = 1
    elif dx:
        loads["x+" if dx < X // 2 else "x-"] = 1
    return loads


def balanced_order():
    rest = [(dy, dz, dx) for dy in range(Y_HI) for dz in range(Z) for dx in range(X)][1:]
    count = len(rest)
    total = {k: sum(link_loads(o)[k] for o in rest) for k in RING_LINKS}
    done, order = dict.fromkeys(RING_LINKS, 0), []
    while rest:
        share = (len(order) + 1) / count

        def cost(offset):
            loads = link_loads(offset)
            return sum(
                (done[k] + loads[k] - total[k] * share) ** 2 * (0.3 if k[0] == "x" else 1.0)
                for k in RING_LINKS
            )

        best = min(rest, key=cost)
        rest.remove(best)
        order.append(best)
        for k, v in link_loads(best).items():
            done[k] += v
    return order


ORDER = balanced_order()


def kernel(
    x_hbm, kv_hbm, table_ref, moved_ref,
    values_ref, scales_ref, mla_values_ref, mla_scales_ref,
    x_ref, staged, landed, kv_landed, rank_vmem, rank_smem,
    in_sem, send_sem, recv_sem, kv_send, kv_recv, rank_sem,
):
    n = Y_HI * Z * X
    rows = x_ref.shape[1]
    me, fs = lax.axis_index("expert"), lax.axis_index("fsdp")
    y_hi, z, x = me // (Z * X), (me // X) % Z, me % X
    y_lo, core = fs // CORE, fs % CORE

    load_x = pltpu.make_async_copy(x_hbm, x_ref, in_sem.at[0])
    load_x.start()
    kv_rows = kv_hbm.shape[0]
    my_kv = kv_landed.at[pl.ds(pl.multiple_of(fs * kv_rows, kv_rows), kv_rows)]
    load_kv = pltpu.make_async_copy(kv_hbm, my_kv, in_sem.at[1])
    load_kv.start()

    ys = [((y_hi + d) % Y_HI) * (Z * X) for d in range(Y_HI)]
    zs = [((z + d) % Z) * X for d in range(Z)]
    xs = [(x + d) % X for d in range(X)]

    def peer(offset):
        return ys[offset[0]] + zs[offset[1]] + xs[offset[2]]

    def negative(offset):
        return (-offset[0] % Y_HI, -offset[1] % Z, -offset[2] % X)

    fs_same = [((y_lo + d) % Y_LO) * CORE + core for d in range(Y_LO)]
    sibling = y_lo * CORE + 1 - core

    barrier = pltpu.get_barrier_semaphore()
    for offset in ORDER:
        pl.semaphore_signal(barrier, inc=1, device_id=(peer(negative(offset)), fs), device_id_type=MESH)
    for d in range(1, Y_LO):
        pl.semaphore_signal(barrier, inc=1, device_id=(me, fs_same[d]), device_id_type=MESH)
    pl.semaphore_signal(barrier, inc=1, device_id=(me, sibling), device_id_type=MESH)

    lane = lax.broadcasted_iota(jnp.int32, (n, n), 1)
    row = lax.broadcasted_iota(jnp.int32, (n, n), 0)
    moved = jnp.sum(jnp.where(lane == row, moved_ref[...], 0), axis=1, keepdims=True)
    layer = lax.broadcasted_iota(jnp.int32, (n, table_ref.shape[1]), 1)
    owners = jnp.sum(jnp.where(layer == moved, table_ref[...], 0), axis=1, keepdims=True)
    wide = lax.broadcasted_iota(jnp.int32, (n, 128), 1)
    position = lax.broadcasted_iota(jnp.int32, (n, 128), 0)
    ranking = jnp.max(jnp.where(owners == wide, position, 0), axis=0, keepdims=True)
    rank_vmem[...] = jnp.broadcast_to(ranking, rank_vmem.shape)
    to_smem = pltpu.make_async_copy(rank_vmem, rank_smem, rank_sem)
    to_smem.start()
    to_smem.wait()
    load_x.wait()
    load_kv.wait()

    pl.semaphore_wait(barrier, len(ORDER) + Y_LO)

    def kv_copy(source, target, dev):
        part = kv_landed.at[pl.ds(pl.multiple_of(source * kv_rows, kv_rows), kv_rows)]
        return pltpu.make_async_remote_copy(
            src_ref=part, dst_ref=part, send_sem=kv_send.at[target], recv_sem=kv_recv.at[source],
            device_id=(me, dev), device_id_type=MESH,
        )

    kv_out = [kv_copy(fs, 0, sibling)] + [kv_copy(fs, d, fs_same[d]) for d in range(1, Y_LO)]

    my_rows = pl.ds(pl.multiple_of(me * rows, 16), rows)
    for i, offset in enumerate(ORDER):
        dest = peer(offset)
        part = pl.ds(i * rows, rows)
        staged[part, :] = x_ref[rank_smem[0, dest]]
        pltpu.make_async_remote_copy(
            src_ref=staged.at[part], dst_ref=landed.at[my_rows], send_sem=send_sem,
            recv_sem=recv_sem.at[me], device_id=(dest, fs), device_id_type=MESH,
        ).start()
        if i == 3:
            for copy in kv_out:
                copy.start()
    landed[my_rows, :] = x_ref[rank_smem[0, me]]

    kv_relay = []
    for d in range(1, Y_LO):
        source = fs_same[d]
        kv_copy(source, 0, fs_same[d]).wait_recv()
        copy = kv_copy(source, Y_LO - 1 + d, sibling)
        copy.start()
        kv_relay.append(copy)
    for d in range(Y_LO):
        source = ((y_lo + d) % Y_LO) * CORE + 1 - core
        kv_copy(source, 0, sibling).wait_recv()

    def scaled(block):
        block = block.astype(jnp.float32)
        top = jnp.max(jnp.max(jnp.abs(block), axis=0, keepdims=True), axis=1, keepdims=True)
        scale = top + EPSILON
        return (block * (1.0 / scale)).astype(jnp.bfloat16), scale

    tall, across = mla_scales_ref.shape
    at = lax.broadcasted_iota(jnp.int32, (tall, across), 0) * across + lax.broadcasted_iota(jnp.int32, (tall, across), 1)
    mla_scales = jnp.zeros((tall, across), jnp.float32)
    for a in range(tall):
        for b in range(across):
            where = (pl.ds(a * BLOCK, BLOCK), pl.ds(b * BLOCK, BLOCK))
            mla_values_ref[where], scale = scaled(kv_landed[where])
            mla_scales = jnp.where(at == a * across + b, scale, mla_scales)
    mla_scales_ref[...] = mla_scales

    group, blocks = 8, 8 * rows // BLOCK
    slots = lax.broadcasted_iota(jnp.int32, scales_ref.shape, 1)

    def one_group(g, scales):
        for s in range(group):
            source = g * group + s

            @pl.when(source != me)
            def _():
                where = pl.ds(pl.multiple_of(source * rows, 16), rows)
                pltpu.make_async_remote_copy(
                    src_ref=landed.at[where], dst_ref=landed.at[where], send_sem=send_sem,
                    recv_sem=recv_sem.at[source], device_id=(source, fs), device_id_type=MESH,
                ).wait_recv()

        for b in range(blocks):
            where = pl.ds(pl.multiple_of((g * blocks + b) * BLOCK, BLOCK), BLOCK)
            values_ref[where, :], scale = scaled(landed[where, :])
            scales = jnp.where(slots == g * blocks + b, scale, scales)
        return scales

    scales_ref[...] = lax.fori_loop(0, n // group, one_group, jnp.zeros(scales_ref.shape, jnp.float32))

    sent = staged.at[pl.ds(0, len(ORDER) * rows)]
    pltpu.make_async_remote_copy(
        src_ref=sent, dst_ref=sent, send_sem=send_sem, recv_sem=recv_sem.at[me],
        device_id=(peer(ORDER[0]), fs), device_id_type=MESH,
    ).wait_send()
    for copy in kv_out + kv_relay:
        copy.wait_send()


def on_device(expert_weights, kv_up_weight, owner_table, moved_experts):
    n, rows, columns = expert_weights.shape
    kv_rows, kv_columns = kv_up_weight.shape
    kv_all = kv_rows * Y_LO * CORE
    whole = n * rows
    vmem = pl.BlockSpec(memory_space=pltpu.VMEM)
    anywhere = pl.BlockSpec(memory_space=pl.ANY)
    values, scales, mla_values, mla_scales = pl.pallas_call(
        kernel,
        out_shape=(
            jax.ShapeDtypeStruct((whole, columns), jnp.bfloat16),
            jax.ShapeDtypeStruct((1, whole // BLOCK), jnp.float32),
            jax.ShapeDtypeStruct((kv_all, kv_columns), jnp.bfloat16),
            jax.ShapeDtypeStruct((kv_all // BLOCK, kv_columns // BLOCK), jnp.float32),
        ),
        in_specs=[anywhere, anywhere, vmem, vmem],
        out_specs=(vmem, vmem, vmem, vmem),
        scratch_shapes=[
            pltpu.VMEM((n, rows, columns), jnp.bfloat16),
            pltpu.VMEM((whole, columns), jnp.bfloat16),
            pltpu.VMEM((whole, columns), jnp.bfloat16),
            pltpu.VMEM((kv_all, kv_columns), jnp.bfloat16),
            pltpu.VMEM((8, 128), jnp.int32),
            pltpu.SMEM((8, 128), jnp.int32),
            pltpu.SemaphoreType.DMA((2,)),
            pltpu.SemaphoreType.DMA,
            pltpu.SemaphoreType.DMA((n,)),
            pltpu.SemaphoreType.DMA((2 * Y_LO,)),
            pltpu.SemaphoreType.DMA((Y_LO * CORE,)),
            pltpu.SemaphoreType.DMA,
        ],
        compiler_params=pltpu.CompilerParams(
            collective_id=0, has_side_effects=True, vmem_limit_bytes=40 << 20
        ),
    )(
        expert_weights, kv_up_weight,
        owner_table.reshape(1, -1), moved_experts.reshape(1, -1),
    )
    return (
        values.reshape(1, whole, columns),
        scales.reshape(1, whole // BLOCK, 1),
        mla_values,
        mla_scales,
    )


def solution(mesh):
    in_specs = (P(None, "expert", "fsdp"), P("fsdp", "expert"), P(), P())
    out_specs = (
        P("expert", None, "fsdp"),
        P("expert", None, "fsdp"),
        P(None, "expert"),
        P(None, "expert"),
    )
    return jax.shard_map(
        on_device, mesh=mesh, in_specs=in_specs, out_specs=out_specs, check_vma=False
    )
```

time: 96.7 us -> 77.2 us (0.80)
  the two profiles are of different devices: /device:TPU:129 before, /device:TPU:32 now
where the time goes in v1:
time: 77.2 us; the launch traced here: 77 us
  Pallas kernels  69.6 us (90%)
  local copies, waits for them, and re-layouts  6.78 us (9%)
    pallas_call x1, Pallas kernels, on_device(): pl.pallas_call(kernel, out_shape=(jax.ShapeDtypeStruct((whole, columns),...  69.6 us
    unnamed x12, local copies, waits for them, and re-layouts  6.78 us

profile of v1, /device:TPU:32, one launch (start us, length us, event | category | flops | bytes accessed | tf_op | source)
XLA Modules:
  0.0 77.0 jit_solution(9273516466313240831)
XLA Ops:
  0.6 0.0 copy-start
  0.6 1.5 %copy-done = bf16[64,112,128]{2,1,0:T(8,128)(2,1)S(1)} copy-done((bf16[64,112,128]{2,1,0:T(8,128)(2,1)S(1)}, bf16[64,112,128]{2,1,0:T(8,128)(2,1)}, u32[]{:S(2)}) %copy-start) | copy-done | bytes 1835032
  2.1 0.0 copy-start.1
  2.1 0.8 %copy-done.1 = bf16[64,512]{1,0:T(8,128)(2,1)S(1)} copy-done((bf16[64,512]{1,0:T(8,128)(2,1)S(1)}, bf16[64,512]{1,0:T(8,128)(2,1)}, u32[]{:S(2)}) %copy-start.1) | copy-done | bytes 65560
  3.0 0.0 copy-start.2
  3.0 0.7 copy-done.2
  3.7 0.0 copy-start.3
  3.7 0.7 copy-done.3
  4.3 69.6 %shard_map.75 = (bf16[7168,128]{1,0:T(8,128)(2,1)S(1)}, f32[1,56]{1,0:T(1,128)S(1)}, bf16[512,512]{1,0:T(8,128)(2,1)S(1)}, f32[4,4]{1,0:T(4,128)S(1)}) custom-call(bf16[64,112,128]{2,1,0:T(8,128)(2,1)S(1)} %copy-done, bf16[64,512]{1,0:T(8,128)(2,1)S(1)} %copy-done.1, s32[1,256]{1,0:T(1,128)S(1)} %bitcast.5, s32[1,64]{1,0:T(1,128)S(1)} %bitcast.6), custom_call_target="tpu_custom_call" | custom-call | tf_op jit(solution)/shard_map/pallas_call | solution.py:205
  73.9 1.2 %copy.12 = bf16[1,7168,128]{2,1,0:T(8,128)(2,1)} copy(bf16[1,7168,128]{2,1,0:T(8,128)(2,1)S(1)} %bitcast.4) | data formatting | bytes 3670016
  75.1 0.5 copy.13
  75.7 0.8 %copy.14 = bf16[512,512]{1,0:T(8,128)(2,1)} copy(bf16[512,512]{1,0:T(8,128)(2,1)S(1)} %get-tuple-element.18) | data formatting | bytes 1048576
  76.4 0.6 copy.15
Async XLA Ops:
  0.6 1.5 %copy-start = (bf16[64,112,128]{2,1,0:T(8,128)(2,1)S(1)}, bf16[64,112,128]{2,1,0:T(8,128)(2,1)}, u32[]{:S(2)}) copy-start(bf16[64,112,128]{2,1,0:T(8,128)(2,1)} %x_hbm.1) | copy-start | bytes 5505028
  2.1 0.8 %copy-start.1 = (bf16[64,512]{1,0:T(8,128)(2,1)S(1)}, bf16[64,512]{1,0:T(8,128)(2,1)}, u32[]{:S(2)}) copy-start(bf16[64,512]{1,0:T(8,128)(2,1)} %kv_hbm.1) | copy-start | bytes 196612
  3.0 0.7 copy-start.2
  3.7 0.7 copy-start.3

commit v2 on v1

--- a/solution.py
+++ b/solution.py
@@ -58,9 +58,9 @@
 
 
 def kernel(
-    x_hbm, kv_hbm, table_ref, moved_ref,
+    x_hbm, kv_hbm, table_hbm, moved_hbm,
     values_ref, scales_ref, mla_values_ref, mla_scales_ref,
-    x_ref, staged, landed, kv_landed, rank_vmem, rank_smem,
+    x_ref, staged, landed, kv_landed, table_ref, moved_ref, rank_vmem, rank_smem,
     in_sem, send_sem, recv_sem, kv_send, kv_recv, rank_sem,
 ):
     n = Y_HI * Z * X
@@ -69,6 +69,10 @@
     y_hi, z, x = me // (Z * X), (me // X) % Z, me % X
     y_lo, core = fs // CORE, fs % CORE
 
+    load_moved = pltpu.make_async_copy(moved_hbm, moved_ref, in_sem.at[2])
+    load_moved.start()
+    load_table = pltpu.make_async_copy(table_hbm, table_ref, in_sem.at[3])
+    load_table.start()
     load_x = pltpu.make_async_copy(x_hbm, x_ref, in_sem.at[0])
     load_x.start()
     kv_rows = kv_hbm.shape[0]
@@ -96,6 +100,8 @@
         pl.semaphore_signal(barrier, inc=1, device_id=(me, fs_same[d]), device_id_type=MESH)
     pl.semaphore_signal(barrier, inc=1, device_id=(me, sibling), device_id_type=MESH)
 
+    load_moved.wait()
+    load_table.wait()
     lane = lax.broadcasted_iota(jnp.int32, (n, n), 1)
     row = lax.broadcasted_iota(jnp.int32, (n, n), 0)
     moved = jnp.sum(jnp.where(lane == row, moved_ref[...], 0), axis=1, keepdims=True)
@@ -195,14 +201,24 @@
         copy.wait_send()
 
 
+def write_out(*refs):
+    half = len(refs) // 2
+    sems = refs[-1]
+    copies = [pltpu.make_async_copy(refs[i], refs[half + i], sems.at[i]) for i in range(half)]
+    for copy in copies:
+        copy.start()
+    for copy in copies:
+        copy.wait()
+
+
 def on_device(expert_weights, kv_up_weight, owner_table, moved_experts):
     n, rows, columns = expert_weights.shape
     kv_rows, kv_columns = kv_up_weight.shape
     kv_all = kv_rows * Y_LO * CORE
     whole = n * rows
     vmem = pl.BlockSpec(memory_space=pltpu.VMEM)
-    anywhere = pl.BlockSpec(memory_space=pl.ANY)
-    values, scales, mla_values, mla_scales = pl.pallas_call(
+    hbm = pl.BlockSpec(memory_space=pltpu.HBM)
+    results = pl.pallas_call(
         kernel,
         out_shape=(
             jax.ShapeDtypeStruct((whole, columns), jnp.bfloat16),
@@ -210,16 +226,18 @@
             jax.ShapeDtypeStruct((kv_all, kv_columns), jnp.bfloat16),
             jax.ShapeDtypeStruct((kv_all // BLOCK, kv_columns // BLOCK), jnp.float32),
         ),
-        in_specs=[anywhere, anywhere, vmem, vmem],
+        in_specs=[hbm] * 4,
         out_specs=(vmem, vmem, vmem, vmem),
         scratch_shapes=[
             pltpu.VMEM((n, rows, columns), jnp.bfloat16),
             pltpu.VMEM((whole, columns), jnp.bfloat16),
             pltpu.VMEM((whole, columns), jnp.bfloat16),
             pltpu.VMEM((kv_all, kv_columns), jnp.bfloat16),
+            pltpu.VMEM((1, owner_table.shape[0]), jnp.int32),
+            pltpu.VMEM((1, n), jnp.int32),
             pltpu.VMEM((8, 128), jnp.int32),
             pltpu.SMEM((8, 128), jnp.int32),
-            pltpu.SemaphoreType.DMA((2,)),
+            pltpu.SemaphoreType.DMA((4,)),
             pltpu.SemaphoreType.DMA,
             pltpu.SemaphoreType.DMA((n,)),
             pltpu.SemaphoreType.DMA((2 * Y_LO,)),
@@ -230,9 +248,18 @@
             collective_id=0, has_side_effects=True, vmem_limit_bytes=40 << 20
         ),
     )(
-        expert_weights, kv_up_weight,
-        owner_table.reshape(1, -1), moved_experts.reshape(1, -1),
-    )
+        *(
+            pltpu.with_memory_space_constraint(a, pltpu.HBM)
+            for a in (expert_weights, kv_up_weight, owner_table.reshape(1, -1), moved_experts.reshape(1, -1))
+        ),
+    )
+    values, scales, mla_values, mla_scales = pl.pallas_call(
+        write_out,
+        out_shape=tuple(jax.ShapeDtypeStruct(r.shape, r.dtype) for r in results),
+        in_specs=[vmem] * 4,
+        out_specs=(hbm,) * 4,
+        scratch_shapes=[pltpu.SemaphoreType.DMA((4,))],
+    )(*results)
     return (
         values.reshape(1, whole, columns),
         scales.reshape(1, whole // BLOCK, 1),

time: 77.2 us -> 76.4 us (0.990)
  local copies, waits for them, and re-layouts: 6.78 us -> 3.15 us
  Pallas kernels: 69.6 us -> 72.4 us
    unnamed x12 -> x8, local copies, waits for them, and re-layouts: 6.78 us -> 3.15 us
    pallas_call x0 -> x1, Pallas kernels: none -> 3.03 us  [on_device(): pl.pallas_call(write_out, out_shape=tuple((jax.ShapeDtypeStruct(r.shape,...]
where the time goes in v2:
time: 76.4 us; the launch traced here: 76.3 us
  Pallas kernels  72.4 us (95%)
  local copies, waits for them, and re-layouts  3.15 us (4%)
    pallas_call x1, Pallas kernels, on_device(): pl.pallas_call(kernel, out_shape=(jax.ShapeDtypeStruct((whole, columns),...  69.4 us
    unnamed x8, local copies, waits for them, and re-layouts  3.15 us
    pallas_call x1, Pallas kernels, on_device(): pl.pallas_call(write_out, out_shape=tuple((jax.ShapeDtypeStruct(r.shape,...  3.03 us

profile of v2, /device:TPU:32, one launch (start us, length us, event | category | flops | bytes accessed | tf_op | source)
XLA Modules:
  0.0 76.3 jit_solution(10799666929220249228)
XLA Ops:
  0.6 69.4 %shard_map.75 = (bf16[7168,128]{1,0:T(8,128)(2,1)S(1)}, f32[1,56]{1,0:T(1,128)S(1)}, bf16[512,512]{1,0:T(8,128)(2,1)S(1)}, f32[4,4]{1,0:T(4,128)S(1)}) custom-call(bf16[64,112,128]{2,1,0:T(8,128)(2,1)} %x_hbm.1, bf16[64,512]{1,0:T(8,128)(2,1)} %kv_hbm.1, s32[1,256]{1,0:T(1,128)} %bitcast.4, s32[1,64]{1,0:T(1,128)} %bitcast.5), custom_call_target="tpu_custom_call" | custom-call | tf_op jit(solution)/shard_map/pallas_call | solution.py:221
  70.1 0.0 copy-start
  70.1 1.2 %copy-done = bf16[7168,128]{1,0:T(8,128)(2,1)} copy-done((bf16[7168,128]{1,0:T(8,128)(2,1)}, bf16[7168,128]{1,0:T(8,128)(2,1)S(1)}, u32[]{:S(2)}) %copy-start) | copy-done | bytes 1835032
  71.3 0.0 copy-start.1
  71.3 0.8 %copy-done.1 = bf16[512,512]{1,0:T(8,128)(2,1)} copy-done((bf16[512,512]{1,0:T(8,128)(2,1)}, bf16[512,512]{1,0:T(8,128)(2,1)S(1)}, u32[]{:S(2)}) %copy-start.1) | copy-done | bytes 524312
  72.1 0.0 copy-start.2
  72.1 0.6 copy-done.2
  72.7 0.0 copy-start.3
  72.7 0.5 copy-done.3
  73.2 3.0 %shard_map.76 = (bf16[7168,128]{1,0:T(8,128)(2,1)}, f32[1,56]{1,0:T(1,128)}, bf16[512,512]{1,0:T(8,128)(2,1)}, f32[4,4]{1,0:T(4,128)}) custom-call(bf16[7168,128]{1,0:T(8,128)(2,1)} %copy-done, f32[1,56]{1,0:T(1,128)} %copy-done.3, bf16[512,512]{1,0:T(8,128)(2,1)} %copy-done.1, f32[4,4]{1,0:T(4,128)} %copy-done.2), custom_call_target="tpu_custom_call" | custom-call | tf_op jit(solution)/shard_map/pallas_call | solution.py:256
Async XLA Ops:
  70.1 1.2 %copy-start = (bf16[7168,128]{1,0:T(8,128)(2,1)}, bf16[7168,128]{1,0:T(8,128)(2,1)S(1)}, u32[]{:S(2)}) copy-start(bf16[7168,128]{1,0:T(8,128)(2,1)S(1)} %get-tuple-element.12.refs_0_) | copy-start | bytes 5505028
  71.3 0.8 %copy-start.1 = (bf16[512,512]{1,0:T(8,128)(2,1)}, bf16[512,512]{1,0:T(8,128)(2,1)S(1)}, u32[]{:S(2)}) copy-start(bf16[512,512]{1,0:T(8,128)(2,1)S(1)} %get-tuple-element.14.refs_2_) | copy-start | bytes 1572868
  72.1 0.6 copy-start.2
  72.7 0.5 copy-start.3

commit v3 on v2

v3 whole, which is shorter than its diff:
```python
import functools

import jax
import jax.numpy as jnp
from jax import lax
from jax.experimental import pallas as pl
from jax.experimental.pallas import tpu as pltpu
from jax.sharding import PartitionSpec as P

MESH = pl.DeviceIdType.MESH
BLOCK = 128
EPSILON = 1e-06
Y_HI, Z, X = 2, 8, 4
Y_LO, CORE = 4, 2
FORWARD = (4, 3, 5, 2, 6, 1, 7, 0)
GATHER_AT = 5


def own_order():
    return [(dz, dx) for dx in range(X) for dz in (4, 3, 5, 2, 6, 1, 7, 0) if dz or dx]


def kernel(
    x_hbm, kv_hbm, table_hbm, moved_hbm,
    values_ref, scales_ref, mla_values_ref, mla_scales_ref,
    x_ref, staged, relayed, landed, kv_landed, table_ref, moved_ref, rank_vmem, rank_smem,
    in_sem, own_send, y_send, relay_send, y_recv, recv_sem, kv_send, kv_recv, rank_sem,
):
    n = Y_HI * Z * X
    rows = x_ref.shape[1]
    me, fs = lax.axis_index("expert"), lax.axis_index("fsdp")
    y_hi, z, x = me // (Z * X), (me // X) % Z, me % X
    y_lo, core = fs // CORE, fs % CORE

    load_moved = pltpu.make_async_copy(moved_hbm, moved_ref, in_sem.at[2])
    load_moved.start()
    load_table = pltpu.make_async_copy(table_hbm, table_ref, in_sem.at[3])
    load_table.start()
    load_x = pltpu.make_async_copy(x_hbm, x_ref, in_sem.at[0])
    load_x.start()
    kv_rows = kv_hbm.shape[0]
    my_kv = kv_landed.at[pl.ds(pl.multiple_of(fs * kv_rows, kv_rows), kv_rows)]
    load_kv = pltpu.make_async_copy(kv_hbm, my_kv, in_sem.at[1])
    load_kv.start()

    here, there = y_hi * (Z * X), (1 - y_hi) * (Z * X)
    zs = [((z + d) % Z) * X for d in range(Z)]
    xs = [(x + d) % X for d in range(X)]
    partner = there + zs[0] + xs[0]
    fs_same = [((y_lo + d) % Y_LO) * CORE + core for d in range(Y_LO)]
    sibling = y_lo * CORE + 1 - core
    near = [(dz, dx) for dz in range(Z) for dx in range(X) if dz or dx]

    barrier = pltpu.get_barrier_semaphore()

    def greet(expert, fsdp):
        pl.semaphore_signal(barrier, inc=1, device_id=(expert, fsdp), device_id_type=MESH)

    greet(partner, fs)
    for dz, dx in near:
        greet(here + zs[dz] + xs[dx], fs)
    for d in range(1, Y_LO):
        greet(me, fs_same[d])
    greet(me, sibling)

    load_moved.wait()
    load_table.wait()
    lane = lax.broadcasted_iota(jnp.int32, (n, n), 1)
    row = lax.broadcasted_iota(jnp.int32, (n, n), 0)
    moved = jnp.sum(jnp.where(lane == row, moved_ref[...], 0), axis=1, keepdims=True)
    layer = lax.broadcasted_iota(jnp.int32, (n, table_ref.shape[1]), 1)
    owners = jnp.sum(jnp.where(layer == moved, table_ref[...], 0), axis=1, keepdims=True)
    wide = lax.broadcasted_iota(jnp.int32, (n, 128), 1)
    position = lax.broadcasted_iota(jnp.int32, (n, 128), 0)
    ranking = jnp.max(jnp.where(owners == wide, position, 0), axis=0, keepdims=True)
    rank_vmem[...] = jnp.broadcast_to(ranking, rank_vmem.shape)
    to_smem = pltpu.make_async_copy(rank_vmem, rank_smem, rank_sem)
    to_smem.start()
    to_smem.wait()
    load_x.wait()
    load_kv.wait()

    def stage(slot, owner):
        staged[pl.ds(slot * rows, rows), :] = x_ref[rank_smem[0, owner]]

    def chunk_copy(j):
        part = pl.ds(j * X * rows, X * rows)
        return pltpu.make_async_remote_copy(
            src_ref=staged.at[part], dst_ref=relayed.at[part], send_sem=y_send,
            recv_sem=y_recv.at[j], device_id=(partner, fs), device_id_type=MESH,
        )

    def block_copy(source, origin, dest, sem):
        to = pl.ds(pl.multiple_of(origin * rows, 16), rows)
        return pltpu.make_async_remote_copy(
            src_ref=source, dst_ref=landed.at[to], send_sem=sem,
            recv_sem=recv_sem.at[origin], device_id=(dest, fs), device_id_type=MESH,
        )

    def kv_copy(source, target, dev):
        part = kv_landed.at[pl.ds(pl.multiple_of(source * kv_rows, kv_rows), kv_rows)]
        return pltpu.make_async_remote_copy(
            src_ref=part, dst_ref=part, send_sem=kv_send.at[target], recv_sem=kv_recv.at[source],
            device_id=(me, dev), device_id_type=MESH,
        )

    def stage_chunk(j):
        for dx in range(X):
            stage(j * X + dx, there + zs[FORWARD[j]] + xs[dx])

    stage_chunk(0)
    pl.semaphore_wait(barrier, 1 + len(near) + Y_LO)
    for j in range(Z):
        if j:
            stage_chunk(j)
        chunk_copy(j).start()
    for i, (dz, dx) in enumerate(own_order()):
        dest = here + zs[dz] + xs[dx]
        stage(Z * X + i, dest)
        block_copy(staged.at[pl.ds((Z * X + i) * rows, rows)], me, dest, own_send).start()
    landed[pl.ds(pl.multiple_of(me * rows, 16), rows), :] = x_ref[rank_smem[0, me]]

    kv_out = [kv_copy(fs, 0, sibling)] + [kv_copy(fs, d, fs_same[d]) for d in range(1, Y_LO)]
    for j, dz in enumerate(FORWARD):
        chunk_copy(j).wait_recv()
        for dx in range(X):
            part = pl.ds((j * X + dx) * rows, rows)
            if dz or dx:
                block_copy(relayed.at[part], partner, here + zs[dz] + xs[dx], relay_send).start()
            else:
                landed[pl.ds(pl.multiple_of(partner * rows, 16), rows), :] = relayed[part, :]
        if j + 1 == GATHER_AT:
            for copy in kv_out:
                copy.start()

    kv_relay = []
    for d in range(1, Y_LO):
        source = fs_same[d]
        kv_copy(source, 0, source).wait_recv()
        copy = kv_copy(source, Y_LO - 1 + d, sibling)
        copy.start()
        kv_relay.append(copy)

    def scaled(block):
        block = block.astype(jnp.float32)
        top = jnp.max(jnp.max(jnp.abs(block), axis=0, keepdims=True), axis=1, keepdims=True)
        scale = top + EPSILON
        return (block * (1.0 / scale)).astype(jnp.bfloat16), scale

    pair = 2 * X
    blocks = pair * rows // BLOCK
    slots = lax.broadcasted_iota(jnp.int32, scales_ref.shape, 1)

    def one_group(half, k, scales):
        first = half + k * pair
        for s in range(pair):
            source = first + s

            @pl.when(jnp.logical_and(source != me, source != partner))
            def _():
                where = landed.at[pl.ds(pl.multiple_of(source * rows, 16), rows)]
                block_copy(where, source, sibling, own_send).wait_recv()

        for b in range(blocks):
            at = first // pair * blocks + b
            where = pl.ds(pl.multiple_of(at * BLOCK, BLOCK), BLOCK)
            values_ref[where, :], scale = scaled(landed[where, :])
            scales = jnp.where(slots == at, scale, scales)
        return scales

    def half_of_groups(half, scales):
        return lax.fori_loop(
            0, Z // 2, lambda k, kept: one_group(half, (z // 2 + 2 + k * 3) % (Z // 2), kept), scales
        )

    scales = half_of_groups(here, jnp.zeros(scales_ref.shape, jnp.float32))

    for d in range(Y_LO):
        source = ((y_lo + d) % Y_LO) * CORE + 1 - core
        kv_copy(source, 0, sibling).wait_recv()
    tall, across = mla_scales_ref.shape
    at = lax.broadcasted_iota(jnp.int32, (tall, across), 0) * across + lax.broadcasted_iota(jnp.int32, (tall, across), 1)
    mla_scales = jnp.zeros((tall, across), jnp.float32)
    for a in range(tall):
        for b in range(across):
            where = (pl.ds(a * BLOCK, BLOCK), pl.ds(b * BLOCK, BLOCK))
            mla_values_ref[where], scale = scaled(kv_landed[where])
            mla_scales = jnp.where(at == a * across + b, scale, mla_scales)
    mla_scales_ref[...] = mla_scales

    scales_ref[...] = half_of_groups(there, scales)

    def all_sent(sem, count):
        sent = staged.at[pl.ds(0, count * rows)]
        pltpu.make_async_remote_copy(
            src_ref=sent, dst_ref=sent, send_sem=sem, recv_sem=recv_sem.at[me],
            device_id=(partner, fs), device_id_type=MESH,
        ).wait_send()

    all_sent(y_send, Z * X)
    all_sent(own_send, Z * X - 1)
    all_sent(relay_send, Z * X - 1)
    for copy in kv_out + kv_relay:
        copy.wait_send()


def write_out(*refs):
    half = len(refs) // 2
    sems = refs[-1]
    copies = [pltpu.make_async_copy(refs[i], refs[half + i], sems.at[i]) for i in range(half)]
    for copy in copies:
        copy.start()
    for copy in copies:
        copy.wait()


def on_device(expert_weights, kv_up_weight, owner_table, moved_experts):
    n, rows, columns = expert_weights.shape
    kv_rows, kv_columns = kv_up_weight.shape
    kv_all = kv_rows * Y_LO * CORE
    whole = n * rows
    vmem = pl.BlockSpec(memory_space=pltpu.VMEM)
    hbm = pl.BlockSpec(memory_space=pltpu.HBM)
    results = pl.pallas_call(
        kernel,
        out_shape=(
            jax.ShapeDtypeStruct((whole, columns), jnp.bfloat16),
            jax.ShapeDtypeStruct((1, whole // BLOCK), jnp.float32),
            jax.ShapeDtypeStruct((kv_all, kv_columns), jnp.bfloat16),
            jax.ShapeDtypeStruct((kv_all // BLOCK, kv_columns // BLOCK), jnp.float32),
        ),
        in_specs=[hbm] * 4,
        out_specs=(vmem, vmem, vmem, vmem),
        scratch_shapes=[
            pltpu.VMEM((n, rows, columns), jnp.bfloat16),
            pltpu.VMEM((whole, columns), jnp.bfloat16),
            pltpu.VMEM((whole // Y_HI, columns), jnp.bfloat16),
            pltpu.VMEM((whole, columns), jnp.bfloat16),
            pltpu.VMEM((kv_all, kv_columns), jnp.bfloat16),
            pltpu.VMEM((1, owner_table.shape[0]), jnp.int32),
            pltpu.VMEM((1, n), jnp.int32),
            pltpu.VMEM((8, 128), jnp.int32),
            pltpu.SMEM((8, 128), jnp.int32),
            pltpu.SemaphoreType.DMA((4,)),
            pltpu.SemaphoreType.DMA,
            pltpu.SemaphoreType.DMA,
            pltpu.SemaphoreType.DMA,
            pltpu.SemaphoreType.DMA((Z,)),
            pltpu.SemaphoreType.DMA((n,)),
            pltpu.SemaphoreType.DMA((2 * Y_LO,)),
            pltpu.SemaphoreType.DMA((Y_LO * CORE,)),
            pltpu.SemaphoreType.DMA,
        ],
        compiler_params=pltpu.CompilerParams(
            collective_id=0, has_side_effects=True, vmem_limit_bytes=40 << 20
        ),
    )(
        *(
            pltpu.with_memory_space_constraint(a, pltpu.HBM)
            for a in (expert_weights, kv_up_weight, owner_table.reshape(1, -1), moved_experts.reshape(1, -1))
        ),
    )
    values, scales, mla_values, mla_scales = pl.pallas_call(
        write_out,
        out_shape=tuple(jax.ShapeDtypeStruct(r.shape, r.dtype) for r in results),
        in_specs=[vmem] * 4,
        out_specs=(hbm,) * 4,
        scratch_shapes=[pltpu.SemaphoreType.DMA((4,))],
    )(*results)
    return (
        values.reshape(1, whole, columns),
        scales.reshape(1, whole // BLOCK, 1),
        mla_values,
        mla_scales,
    )


def solution(mesh):
    in_specs = (P(None, "expert", "fsdp"), P("fsdp", "expert"), P(), P())
    out_specs = (
        P("expert", None, "fsdp"),
        P("expert", None, "fsdp"),
        P(None, "expert"),
        P(None, "expert"),
    )
    return jax.shard_map(
        on_device, mesh=mesh, in_specs=in_specs, out_specs=out_specs, check_vma=False
    )
```

time: 76.4 us -> 71.1 us (0.931)
  the two profiles are of different devices: /device:TPU:32 before, /device:TPU:57 now
where the time goes in v3:
time: 71.1 us; the launch traced here: 70.9 us
  Pallas kernels  67.1 us (94%)
  local copies, waits for them, and re-layouts  3.15 us (4%)
    pallas_call x1, Pallas kernels, on_device(): pl.pallas_call(kernel, out_shape=(jax.ShapeDtypeStruct((whole, columns),...  64.1 us
    unnamed x8, local copies, waits for them, and re-layouts  3.15 us
    pallas_call x1, Pallas kernels, on_device(): pl.pallas_call(write_out, out_shape=tuple((jax.ShapeDtypeStruct(r.shape,...  3.03 us

profile of v3, /device:TPU:57, one launch (start us, length us, event | category | flops | bytes accessed | tf_op | source)
XLA Modules:
  0.0 70.9 jit_solution(14940702224078299600)
XLA Ops:
  0.6 64.1 %shard_map.75 = (bf16[7168,128]{1,0:T(8,128)(2,1)S(1)}, f32[1,56]{1,0:T(1,128)S(1)}, bf16[512,512]{1,0:T(8,128)(2,1)S(1)}, f32[4,4]{1,0:T(4,128)S(1)}) custom-call(bf16[64,112,128]{2,1,0:T(8,128)(2,1)} %x_hbm.1, bf16[64,512]{1,0:T(8,128)(2,1)} %kv_hbm.1, s32[1,256]{1,0:T(1,128)} %bitcast.4, s32[1,64]{1,0:T(1,128)} %bitcast.5), custom_call_target="tpu_custom_call" | custom-call | tf_op jit(solution)/shard_map/pallas_call | solution.py:224
  64.7 0.0 copy-start
  64.7 1.2 %copy-done = bf16[7168,128]{1,0:T(8,128)(2,1)} copy-done((bf16[7168,128]{1,0:T(8,128)(2,1)}, bf16[7168,128]{1,0:T(8,128)(2,1)S(1)}, u32[]{:S(2)}) %copy-start) | copy-done | bytes 1835032
  66.0 0.0 copy-start.1
  66.0 0.8 %copy-done.1 = bf16[512,512]{1,0:T(8,128)(2,1)} copy-done((bf16[512,512]{1,0:T(8,128)(2,1)}, bf16[512,512]{1,0:T(8,128)(2,1)S(1)}, u32[]{:S(2)}) %copy-start.1) | copy-done | bytes 524312
  66.8 0.0 copy-start.2
  66.8 0.6 copy-done.2
  67.4 0.0 copy-start.3
  67.4 0.5 copy-done.3
  67.9 3.0 %shard_map.76 = (bf16[7168,128]{1,0:T(8,128)(2,1)}, f32[1,56]{1,0:T(1,128)}, bf16[512,512]{1,0:T(8,128)(2,1)}, f32[4,4]{1,0:T(4,128)}) custom-call(bf16[7168,128]{1,0:T(8,128)(2,1)} %copy-done, f32[1,56]{1,0:T(1,128)} %copy-done.3, bf16[512,512]{1,0:T(8,128)(2,1)} %copy-done.1, f32[4,4]{1,0:T(4,128)} %copy-done.2), custom_call_target="tpu_custom_call" | custom-call | tf_op jit(solution)/shard_map/pallas_call | solution.py:263
Async XLA Ops:
  64.7 1.2 %copy-start = (bf16[7168,128]{1,0:T(8,128)(2,1)}, bf16[7168,128]{1,0:T(8,128)(2,1)S(1)}, u32[]{:S(2)}) copy-start(bf16[7168,128]{1,0:T(8,128)(2,1)S(1)} %get-tuple-element.12.refs_0_) | copy-start | bytes 5505028
  66.0 0.8 %copy-start.1 = (bf16[512,512]{1,0:T(8,128)(2,1)}, bf16[512,512]{1,0:T(8,128)(2,1)S(1)}, u32[]{:S(2)}) copy-start(bf16[512,512]{1,0:T(8,128)(2,1)S(1)} %get-tuple-element.14.refs_2_) | copy-start | bytes 1572868
  66.8 0.6 copy-start.2
  67.4 0.5 copy-start.3

commit v4 on v3

--- a/solution.py
+++ b/solution.py
@@ -24,7 +24,7 @@
     x_hbm, kv_hbm, table_hbm, moved_hbm,
     values_ref, scales_ref, mla_values_ref, mla_scales_ref,
     x_ref, staged, relayed, landed, kv_landed, table_ref, moved_ref, rank_vmem, rank_smem,
-    in_sem, own_send, y_send, relay_send, y_recv, recv_sem, kv_send, kv_recv, rank_sem,
+    in_sem, own_send, y_send, relay_send, y_recv, recv_sem, kv_send, kv_recv, rank_sem, ready,
 ):
     n = Y_HI * Z * X
     rows = x_ref.shape[1]
@@ -49,7 +49,12 @@
     partner = there + zs[0] + xs[0]
     fs_same = [((y_lo + d) % Y_LO) * CORE + core for d in range(Y_LO)]
     sibling = y_lo * CORE + 1 - core
-    near = [(dz, dx) for dz in range(Z) for dx in range(X) if dz or dx]
+    half = Z // 2
+    upper = z // half
+    planes = half * X
+    low, high = here, here + planes
+    mine, others = here + upper * planes, here + (1 - upper) * planes
+    steps = [((z + d) % half) * X for d in range(half)]
 
     barrier = pltpu.get_barrier_semaphore()
 
@@ -57,8 +62,16 @@
         pl.semaphore_signal(barrier, inc=1, device_id=(expert, fsdp), device_id_type=MESH)
 
     greet(partner, fs)
-    for dz, dx in near:
-        greet(here + zs[dz] + xs[dx], fs)
+
+    @pl.when(upper == 0)
+    def _():
+        for k in range(planes):
+            greet(others + k, fs)
+
+    for d in range(half):
+        for dx in range(X):
+            if d or dx:
+                greet(mine + steps[d] + xs[dx], fs)
     for d in range(1, Y_LO):
         greet(me, fs_same[d])
     greet(me, sibling)
@@ -109,15 +122,39 @@
             stage(j * X + dx, there + zs[FORWARD[j]] + xs[dx])
 
     stage_chunk(0)
-    pl.semaphore_wait(barrier, 1 + len(near) + Y_LO)
+    pl.semaphore_wait(barrier, planes + Y_LO + planes * upper)
+
+    @pl.when(upper == 1)
+    def _():
+        for k in range(planes):
+            pl.semaphore_signal(ready, inc=1, device_id=(others + k, fs), device_id_type=MESH)
+
     for j in range(Z):
         if j:
             stage_chunk(j)
         chunk_copy(j).start()
-    for i, (dz, dx) in enumerate(own_order()):
-        dest = here + zs[dz] + xs[dx]
-        stage(Z * X + i, dest)
-        block_copy(staged.at[pl.ds((Z * X + i) * rows, rows)], me, dest, own_send).start()
+
+    def send_own(slot, dest):
+        stage(slot, dest)
+        block_copy(staged.at[pl.ds(slot * rows, rows)], me, dest, own_send).start()
+
+    @pl.when(upper == 0)
+    def _():
+        slot = Z * X
+        for first in (low, high):
+            if first is high:
+                pl.semaphore_wait(ready, planes)
+            for dx in range(X):
+                for d in (0, 2, 1, 3):
+                    if d or dx or first is high:
+                        send_own(slot, first + steps[d] + xs[dx])
+                        slot += 1
+
+    @pl.when(upper == 1)
+    def _():
+        for i, (dz, dx) in enumerate(own_order()):
+            send_own(Z * X + i, here + zs[dz] + xs[dx])
+
     landed[pl.ds(pl.multiple_of(me * rows, 16), rows), :] = x_ref[rank_smem[0, me]]
 
     kv_out = [kv_copy(fs, 0, sibling)] + [kv_copy(fs, d, fs_same[d]) for d in range(1, Y_LO)]
@@ -151,8 +188,8 @@
     blocks = pair * rows // BLOCK
     slots = lax.broadcasted_iota(jnp.int32, scales_ref.shape, 1)
 
-    def one_group(half, k, scales):
-        first = half + k * pair
+    def one_group(side, k, scales):
+        first = side + k * pair
         for s in range(pair):
             source = first + s
 
@@ -168,9 +205,9 @@
             scales = jnp.where(slots == at, scale, scales)
         return scales
 
-    def half_of_groups(half, scales):
+    def half_of_groups(side, scales):
         return lax.fori_loop(
-            0, Z // 2, lambda k, kept: one_group(half, (z // 2 + 2 + k * 3) % (Z // 2), kept), scales
+            0, Z // 2, lambda k, kept: one_group(side, (z // 2 + 2 + k * 3) % (Z // 2), kept), scales
         )
 
     scales = half_of_groups(here, jnp.zeros(scales_ref.shape, jnp.float32))
@@ -250,6 +287,7 @@
             pltpu.SemaphoreType.DMA((2 * Y_LO,)),
             pltpu.SemaphoreType.DMA((Y_LO * CORE,)),
             pltpu.SemaphoreType.DMA,
+            pltpu.SemaphoreType.REGULAR,
         ],
         compiler_params=pltpu.CompilerParams(
             collective_id=0, has_side_effects=True, vmem_limit_bytes=40 << 20
@@ -263,10 +301,11 @@
     values, scales, mla_values, mla_scales = pl.pallas_call(
         write_out,
         out_shape=tuple(jax.ShapeDtypeStruct(r.shape, r.dtype) for r in results),
-        in_specs=[vmem] * 4,
+        in_specs=[pl.BlockSpec(memory_space=pl.ANY)] * 4,
         out_specs=(hbm,) * 4,
         scratch_shapes=[pltpu.SemaphoreType.DMA((4,))],
-    )(*results)
+        compiler_params=pltpu.CompilerParams(vmem_limit_bytes=1 << 20),
+    )(*(pltpu.with_memory_space_constraint(r, pltpu.VMEM) for r in results))
     return (
         values.reshape(1, whole, columns),
         scales.reshape(1, whole // BLOCK, 1),

time: 71.1 us -> 63.3 us (0.89)
  Pallas kernels: 67.1 us -> 62.5 us
  local copies, waits for them, and re-layouts: 3.15 us -> 0 us
    unnamed x8 -> x0, local copies, waits for them, and re-layouts: 3.15 us -> none
    pallas_call x1, Pallas kernels: 64.1 us -> 61.1 us  [on_device(): pl.pallas_call(kernel, out_shape=(jax.ShapeDtypeStruct((whole, columns),...]
    pallas_call x1, Pallas kernels: 3.03 us -> 1.44 us  [on_device(): pl.pallas_call(write_out, out_shape=tuple((jax.ShapeDtypeStruct(r.shape,...]
where the time goes in v4:
time: 63.3 us; the launch traced here: 63.2 us
  Pallas kernels  62.5 us (99%)
  between operations  0.64 us (1%)
    pallas_call x1, Pallas kernels, on_device(): pl.pallas_call(kernel, out_shape=(jax.ShapeDtypeStruct((whole, columns),...  61.1 us
    pallas_call x1, Pallas kernels, on_device(): pl.pallas_call(write_out, out_shape=tuple((jax.ShapeDtypeStruct(r.shape,...  1.44 us

profile of v4, /device:TPU:57, one launch (start us, length us, event | category | flops | bytes accessed | tf_op | source)
XLA Modules:
  0.0 63.2 jit_solution(1261989561782096518)
XLA Ops:
  0.6 61.1 %shard_map.75 = (bf16[7168,128]{1,0:T(8,128)(2,1)S(1)}, f32[1,56]{1,0:T(1,128)S(1)}, bf16[512,512]{1,0:T(8,128)(2,1)S(1)}, f32[4,4]{1,0:T(4,128)S(1)}) custom-call(bf16[64,112,128]{2,1,0:T(8,128)(2,1)} %x_hbm.1, bf16[64,512]{1,0:T(8,128)(2,1)} %kv_hbm.1, s32[1,256]{1,0:T(1,128)} %bitcast.4, s32[1,64]{1,0:T(1,128)} %bitcast.5), custom_call_target="tpu_custom_call" | custom-call | tf_op jit(solution)/shard_map/pallas_call | solution.py:261
  61.7 1.4 %shard_map.76 = (bf16[7168,128]{1,0:T(8,128)(2,1)}, f32[1,56]{1,0:T(1,128)}, bf16[512,512]{1,0:T(8,128)(2,1)}, f32[4,4]{1,0:T(4,128)}) custom-call(bf16[7168,128]{1,0:T(8,128)(2,1)S(1)} %get-tuple-element.12.refs_0_, f32[1,56]{1,0:T(1,128)S(1)} %get-tuple-element.13.refs_1_, bf16[512,512]{1,0:T(8,128)(2,1)S(1)} %get-tuple-element.14.refs_2_, ...), custom_call_target="tpu_custom_call" | custom-call | tf_op jit(solution)/shard_map/pallas_call | solution.py:301

commit v5 on v4

--- a/solution.py
+++ b/solution.py
@@ -13,18 +13,16 @@
 Y_HI, Z, X = 2, 8, 4
 Y_LO, CORE = 4, 2
 FORWARD = (4, 3, 5, 2, 6, 1, 7, 0)
+IN_FLIGHT = 3
 GATHER_AT = 5
-
-
-def own_order():
-    return [(dz, dx) for dx in range(X) for dz in (4, 3, 5, 2, 6, 1, 7, 0) if dz or dx]
+SPREAD = (0, 2, 1, 3)
 
 
 def kernel(
     x_hbm, kv_hbm, table_hbm, moved_hbm,
     values_ref, scales_ref, mla_values_ref, mla_scales_ref,
     x_ref, staged, relayed, landed, kv_landed, table_ref, moved_ref, rank_vmem, rank_smem,
-    in_sem, own_send, y_send, relay_send, y_recv, recv_sem, kv_send, kv_recv, rank_sem, ready,
+    in_sem, own_send, y_send, relay_send, y_recv, recv_sem, kv_send, kv_recv, rank_sem, partner_ready, plane_ready, gather_ready,
 ):
     n = Y_HI * Z * X
     rows = x_ref.shape[1]
@@ -50,31 +48,45 @@
     fs_same = [((y_lo + d) % Y_LO) * CORE + core for d in range(Y_LO)]
     sibling = y_lo * CORE + 1 - core
     half = Z // 2
-    upper = z // half
     planes = half * X
-    low, high = here, here + planes
-    mine, others = here + upper * planes, here + (1 - upper) * planes
-    steps = [((z + d) % half) * X for d in range(half)]
+    index = z * X + x
+    spread = [(z + d) % half for d in SPREAD]
+    late = y_lo + y_hi * (Y_LO - 1 - 2 * y_lo)
+    lates = [fs_same[d] // CORE + y_hi * (Y_LO - 1 - 2 * (fs_same[d] // CORE)) for d in range(Y_LO)]
 
     barrier = pltpu.get_barrier_semaphore()
 
-    def greet(expert, fsdp):
-        pl.semaphore_signal(barrier, inc=1, device_id=(expert, fsdp), device_id_type=MESH)
-
-    greet(partner, fs)
-
-    @pl.when(upper == 0)
-    def _():
-        for k in range(planes):
-            greet(others + k, fs)
-
-    for d in range(half):
-        for dx in range(X):
-            if d or dx:
-                greet(mine + steps[d] + xs[dx], fs)
+    def signal(sem, expert, fsdp):
+        pl.semaphore_signal(sem, inc=1, device_id=(expert, fsdp), device_id_type=MESH)
+
+    def wait_for(sem, count):
+        @pl.when(count > 0)
+        def _():
+            pl.semaphore_wait(sem, count)
+
+    @pl.when(y_hi == 0)
+    def _():
+        signal(barrier, partner, fs)
+
+    @pl.loop(index + 1, Z * X)
+    def _(k):
+        signal(barrier, here + k, fs)
+
     for d in range(1, Y_LO):
-        greet(me, fs_same[d])
-    greet(me, sibling)
+
+        @pl.when(lates[d] > late)
+        def _():
+            signal(barrier, me, fs_same[d])
+
+    @pl.when(core == 0)
+    def _():
+        signal(barrier, me, sibling)
+
+    wait_for(barrier, index + y_hi + late + core)
+
+    @pl.when(y_hi == 1)
+    def _():
+        signal(partner_ready, partner, fs)
 
     load_moved.wait()
     load_table.wait()
@@ -121,45 +133,87 @@
         for dx in range(X):
             stage(j * X + dx, there + zs[FORWARD[j]] + xs[dx])
 
-    stage_chunk(0)
-    pl.semaphore_wait(barrier, planes + Y_LO + planes * upper)
-
-    @pl.when(upper == 1)
-    def _():
-        for k in range(planes):
-            pl.semaphore_signal(ready, inc=1, device_id=(others + k, fs), device_id_type=MESH)
-
-    for j in range(Z):
-        if j:
-            stage_chunk(j)
+    for j in range(IN_FLIGHT):
+        stage_chunk(j)
+    wait_for(partner_ready, 1 - y_hi)
+    for j in range(IN_FLIGHT):
         chunk_copy(j).start()
 
-    def send_own(slot, dest):
+    @pl.loop(0, index)
+    def _(k):
+        signal(plane_ready.at[z], here + k, fs)
+
+    for d in range(1, Y_LO):
+
+        @pl.when(lates[d] < late)
+        def _():
+            signal(gather_ready, me, fs_same[d])
+
+    @pl.when(core == 1)
+    def _():
+        signal(gather_ready, me, sibling)
+
+    for j in range(IN_FLIGHT, Z):
+        stage_chunk(j)
+
+    def send_own(slot, plane, dx):
+        dest = here + plane * X + xs[dx]
         stage(slot, dest)
         block_copy(staged.at[pl.ds(slot * rows, rows)], me, dest, own_send).start()
 
-    @pl.when(upper == 0)
+    @pl.when(z < half)
     def _():
         slot = Z * X
-        for first in (low, high):
-            if first is high:
-                pl.semaphore_wait(ready, planes)
+        wait_for(plane_ready.at[z], X - 1 - x)
+        for dx in range(1, X):
+            send_own(slot, z, dx)
+            slot += 1
+        for d in (1, 3, 2):
+            plane = (z + d) % half
+
+            @pl.when(plane > z)
+            def _():
+                pl.semaphore_wait(plane_ready.at[plane], X)
+
             for dx in range(X):
-                for d in (0, 2, 1, 3):
-                    if d or dx or first is high:
-                        send_own(slot, first + steps[d] + xs[dx])
-                        slot += 1
-
-    @pl.when(upper == 1)
-    def _():
-        for i, (dz, dx) in enumerate(own_order()):
-            send_own(Z * X + i, here + zs[dz] + xs[dx])
+                send_own(slot, plane, dx)
+                slot += 1
+        for plane in range(half, Z):
+            pl.semaphore_wait(plane_ready.at[plane], X)
+        for dx in range(X):
+            for plane in spread:
+                send_own(slot, half + plane, dx)
+                slot += 1
+
+    @pl.when(z >= half)
+    def _():
+        slot = Z * X
+        for dx in range(X):
+            for plane in spread:
+                send_own(slot, plane, dx)
+                slot += 1
+        wait_for(plane_ready.at[z], X - 1 - x)
+        for plane in range(half + 1, Z):
+
+            @pl.when(plane > z)
+            def _():
+                pl.semaphore_wait(plane_ready.at[plane], X)
+
+        for dx in range(X):
+            for plane in spread[1:]:
+                send_own(slot, half + plane, dx)
+                slot += 1
+        for dx in range(1, X):
+            send_own(slot, z, dx)
+            slot += 1
 
     landed[pl.ds(pl.multiple_of(me * rows, 16), rows), :] = x_ref[rank_smem[0, me]]
 
     kv_out = [kv_copy(fs, 0, sibling)] + [kv_copy(fs, d, fs_same[d]) for d in range(1, Y_LO)]
     for j, dz in enumerate(FORWARD):
         chunk_copy(j).wait_recv()
+        if j + IN_FLIGHT < Z:
+            chunk_copy(j + IN_FLIGHT).start()
         for dx in range(X):
             part = pl.ds((j * X + dx) * rows, rows)
             if dz or dx:
@@ -167,6 +221,7 @@
             else:
                 landed[pl.ds(pl.multiple_of(partner * rows, 16), rows), :] = relayed[part, :]
         if j + 1 == GATHER_AT:
+            wait_for(gather_ready, Y_LO - late - core)
             for copy in kv_out:
                 copy.start()
 
@@ -288,6 +343,8 @@
             pltpu.SemaphoreType.DMA((Y_LO * CORE,)),
             pltpu.SemaphoreType.DMA,
             pltpu.SemaphoreType.REGULAR,
+            pltpu.SemaphoreType.REGULAR((Z,)),
+            pltpu.SemaphoreType.REGULAR,
         ],
         compiler_params=pltpu.CompilerParams(
             collective_id=0, has_side_effects=True, vmem_limit_bytes=40 << 20

time: 63.3 us -> 62.9 us (level)
  the two profiles are of different devices: /device:TPU:57 before, /device:TPU:8 now
where the time goes in v5:
time: 62.9 us; the launch traced here: 62.8 us
  Pallas kernels  62.1 us (99%)
  between operations  0.64 us (1%)
    pallas_call x1, Pallas kernels, on_device(): pl.pallas_call(kernel, out_shape=(jax.ShapeDtypeStruct((whole, columns),...  60.7 us
    pallas_call x1, Pallas kernels, on_device(): pl.pallas_call(write_out, out_shape=tuple((jax.ShapeDtypeStruct(r.shape,...  1.44 us

profile of v5, /device:TPU:8, one launch (start us, length us, event | category | flops | bytes accessed | tf_op | source)
XLA Modules:
  0.0 62.8 jit_solution(7205789424716947582)
XLA Ops:
  0.6 60.7 %shard_map.75 = (bf16[7168,128]{1,0:T(8,128)(2,1)S(1)}, f32[1,56]{1,0:T(1,128)S(1)}, bf16[512,512]{1,0:T(8,128)(2,1)S(1)}, f32[4,4]{1,0:T(4,128)S(1)}) custom-call(bf16[64,112,128]{2,1,0:T(8,128)(2,1)} %x_hbm.1, bf16[64,512]{1,0:T(8,128)(2,1)} %kv_hbm.1, s32[1,256]{1,0:T(1,128)} %bitcast.4, s32[1,64]{1,0:T(1,128)} %bitcast.5), custom_call_target="tpu_custom_call" | custom-call | tf_op jit(solution)/shard_map/pallas_call | solution.py:316
  61.3 1.4 %shard_map.76 = (bf16[7168,128]{1,0:T(8,128)(2,1)}, f32[1,56]{1,0:T(1,128)}, bf16[512,512]{1,0:T(8,128)(2,1)}, f32[4,4]{1,0:T(4,128)}) custom-call(bf16[7168,128]{1,0:T(8,128)(2,1)S(1)} %get-tuple-element.12.refs_0_, f32[1,56]{1,0:T(1,128)S(1)} %get-tuple-element.13.refs_1_, bf16[512,512]{1,0:T(8,128)(2,1)S(1)} %get-tuple-element.14.refs_2_, ...), custom_call_target="tpu_custom_call" | custom-call | tf_op jit(solution)/shard_map/pallas_call | solution.py:358

commit v6 on v5

--- a/solution.py
+++ b/solution.py
@@ -13,6 +13,7 @@
 Y_HI, Z, X = 2, 8, 4
 Y_LO, CORE = 4, 2
 FORWARD = (4, 3, 5, 2, 6, 1, 7, 0)
+FORWARD_LAST = (4, 3, 1, 5, 2, 6, 7, 0)
 IN_FLIGHT = 3
 GATHER_AT = 5
 SPREAD = (0, 2, 1, 3)
@@ -42,9 +43,10 @@
     load_kv.start()
 
     here, there = y_hi * (Z * X), (1 - y_hi) * (Z * X)
-    zs = [((z + d) % Z) * X for d in range(Z)]
+    last = z // (Z - 1)
+    forward = [((z + a + last * (b - a)) % Z) * X for a, b in zip(FORWARD, FORWARD_LAST)]
     xs = [(x + d) % X for d in range(X)]
-    partner = there + zs[0] + xs[0]
+    partner = there + z * X + x
     fs_same = [((y_lo + d) % Y_LO) * CORE + core for d in range(Y_LO)]
     sibling = y_lo * CORE + 1 - core
     half = Z // 2
@@ -131,7 +133,7 @@
 
     def stage_chunk(j):
         for dx in range(X):
-            stage(j * X + dx, there + zs[FORWARD[j]] + xs[dx])
+            stage(j * X + dx, there + forward[j] + xs[dx])
 
     for j in range(IN_FLIGHT):
         stage_chunk(j)
@@ -217,7 +219,7 @@
         for dx in range(X):
             part = pl.ds((j * X + dx) * rows, rows)
             if dz or dx:
-                block_copy(relayed.at[part], partner, here + zs[dz] + xs[dx], relay_send).start()
+                block_copy(relayed.at[part], partner, here + forward[j] + xs[dx], relay_send).start()
             else:
                 landed[pl.ds(pl.multiple_of(partner * rows, 16), rows), :] = relayed[part, :]
         if j + 1 == GATHER_AT:

time: 62.9 us -> 61.5 us (0.978)
  the two profiles are of different devices: /device:TPU:8 before, /device:TPU:79 now
where the time goes in v6:
time: 61.5 us; the launch traced here: 61.3 us
  Pallas kernels  60.7 us (99%)
  between operations  0.64 us (1%)
    pallas_call x1, Pallas kernels, on_device(): pl.pallas_call(kernel, out_shape=(jax.ShapeDtypeStruct((whole, columns),...  59.2 us
    pallas_call x1, Pallas kernels, on_device(): pl.pallas_call(write_out, out_shape=tuple((jax.ShapeDtypeStruct(r.shape,...  1.44 us

profile of v6, /device:TPU:79, one launch (start us, length us, event | category | flops | bytes accessed | tf_op | source)
XLA Modules:
  0.0 61.3 jit_solution(1398232160676430934)
XLA Ops:
  0.6 59.2 %shard_map.75 = (bf16[7168,128]{1,0:T(8,128)(2,1)S(1)}, f32[1,56]{1,0:T(1,128)S(1)}, bf16[512,512]{1,0:T(8,128)(2,1)S(1)}, f32[4,4]{1,0:T(4,128)S(1)}) custom-call(bf16[64,112,128]{2,1,0:T(8,128)(2,1)} %x_hbm.1, bf16[64,512]{1,0:T(8,128)(2,1)} %kv_hbm.1, s32[1,256]{1,0:T(1,128)} %bitcast.4, s32[1,64]{1,0:T(1,128)} %bitcast.5), custom_call_target="tpu_custom_call" | custom-call | tf_op jit(solution)/shard_map/pallas_call | solution.py:318
  59.9 1.4 %shard_map.76 = (bf16[7168,128]{1,0:T(8,128)(2,1)}, f32[1,56]{1,0:T(1,128)}, bf16[512,512]{1,0:T(8,128)(2,1)}, f32[4,4]{1,0:T(4,128)}) custom-call(bf16[7168,128]{1,0:T(8,128)(2,1)S(1)} %get-tuple-element.12.refs_0_, f32[1,56]{1,0:T(1,128)S(1)} %get-tuple-element.13.refs_1_, bf16[512,512]{1,0:T(8,128)(2,1)S(1)} %get-tuple-element.14.refs_2_, ...), custom_call_target="tpu_custom_call" | custom-call | tf_op jit(solution)/shard_map/pallas_call | solution.py:360

commit v7 on v6

--- a/solution.py
+++ b/solution.py
@@ -13,9 +13,9 @@
 Y_HI, Z, X = 2, 8, 4
 Y_LO, CORE = 4, 2
 FORWARD = (4, 3, 5, 2, 6, 1, 7, 0)
-FORWARD_LAST = (4, 3, 1, 5, 2, 6, 7, 0)
+FORWARD_LAST = (4, 3, 5, 1, 2, 6, 7, 0)
 IN_FLIGHT = 3
-GATHER_AT = 5
+GATHER_AT = 6
 SPREAD = (0, 2, 1, 3)
 
 

time: 61.5 us -> 61.5 us (level)
  no operation moved by 1% of the time
where the time goes in v7:
time: 61.5 us; the launch traced here: 61.3 us
  Pallas kernels  60.7 us (99%)
  between operations  0.64 us (1%)
    pallas_call x1, Pallas kernels, on_device(): pl.pallas_call(kernel, out_shape=(jax.ShapeDtypeStruct((whole, columns),...  59.2 us
    pallas_call x1, Pallas kernels, on_device(): pl.pallas_call(write_out, out_shape=tuple((jax.ShapeDtypeStruct(r.shape,...  1.44 us

profile of v7, /device:TPU:79, one launch (start us, length us, event | category | flops | bytes accessed | tf_op | source)
XLA Modules:
  0.0 61.3 jit_solution(11916233674349783712)
XLA Ops:
  0.6 59.2 %shard_map.75 = (bf16[7168,128]{1,0:T(8,128)(2,1)S(1)}, f32[1,56]{1,0:T(1,128)S(1)}, bf16[512,512]{1,0:T(8,128)(2,1)S(1)}, f32[4,4]{1,0:T(4,128)S(1)}) custom-call(bf16[64,112,128]{2,1,0:T(8,128)(2,1)} %x_hbm.1, bf16[64,512]{1,0:T(8,128)(2,1)} %kv_hbm.1, s32[1,256]{1,0:T(1,128)} %bitcast.4, s32[1,64]{1,0:T(1,128)} %bitcast.5), custom_call_target="tpu_custom_call" | custom-call | tf_op jit(solution)/shard_map/pallas_call | solution.py:318
  59.9 1.4 %shard_map.76 = (bf16[7168,128]{1,0:T(8,128)(2,1)}, f32[1,56]{1,0:T(1,128)}, bf16[512,512]{1,0:T(8,128)(2,1)}, f32[4,4]{1,0:T(4,128)}) custom-call(bf16[7168,128]{1,0:T(8,128)(2,1)S(1)} %get-tuple-element.12.refs_0_, f32[1,56]{1,0:T(1,128)S(1)} %get-tuple-element.13.refs_1_, bf16[512,512]{1,0:T(8,128)(2,1)S(1)} %get-tuple-element.14.refs_2_, ...), custom_call_target="tpu_custom_call" | custom-call | tf_op jit(solution)/shard_map/pallas_call | solution.py:360
